TPU v7x, 32 devices: a whole 2x2x4 slice. The times are simulated.
32 devices in a mesh: groups: 1, ep: 16 (over z, y, x), side: 2 (over core).
Axes of the slice: x: 2, y: 2, z: 4, core: 2. Of those that a mesh axis runs over, the one named last changes fastest.
Arguments:
- queries: bfloat16 [128, 128, 576], P(('groups', 'ep', 'side')), may hold values from -16 to 16
- latent_cache: bfloat16 [64, 128, 576], P(('groups', 'ep', 'side')), may hold values from -16 to 16
- new_latent: bfloat16 [128, 576], P(('groups', 'ep', 'side')), may hold values from -6 to 6
- lengths: int32 [64], P(('groups', 'ep', 'side')), may hold values from 2 to 128
- residual: bfloat16 [128, 3584], P(('groups', 'ep', 'side')), may hold values from -6 to 6
- norm_gain: float32 [3584], replicated, may hold values from 0.5 to 1.5
- value_up: bfloat16 [128, 512, 128], P(('ep', 'side')), may hold values from -0.25 to 0.25
- output_proj: bfloat16 [128, 128, 3584], P(('ep', 'side')), may hold values from -0.1875 to 0.1875
- expert_ids: int32 [128, 8], P(('groups', 'ep', 'side')), may hold values from 0 to 15, all different within a row; in each aligned block of 4 rows (0 to 3, 4 to 7, ...) at most 2 rows name the same one
- expert_weights: float32 [128, 8], P(('groups', 'ep', 'side')), may hold values from 0.05 to 0.4
- gate_proj: bfloat16 [16, 3584, 1024], P('ep', None, 'side'), may hold values from -0.09375 to 0.09375
- up_proj: bfloat16 [16, 3584, 1024], P('ep', None, 'side'), may hold values from -0.09375 to 0.09375
- down_proj: bfloat16 [16, 1024, 3584], P('ep', 'side'), may hold values from -0.1875 to 0.1875
Outputs:
- layer_out: bfloat16 [128, 3584], P(('groups', 'ep', 'side'))
Inputs may be any that keep to these rules, and one draw needn't show every extreme that they name: `expert_ids`: each row names 8 different experts. The 4 rows of one device name any one expert at most 2 times, and in every draw some device's rows name some expert exactly 2 times.
All inputs are finite; a program needn't handle non-finite values.
Results may differ from a plain program's by a relative error of at most 0.0056.
Values may be sent and summed in bfloat16 or wider, within the bound.
A program may use at most 64 MiB of HBM per device.

v0:
```python
import jax
import jax.numpy as jnp
from jax import lax
from jax.sharding import PartitionSpec as P

LAT = 512
QKD = 192


norm_epsilon = 1e-06
masked_score = -1e30


def attend_block(query_steps, latent_cache, new_steps, lengths):
    factor = 1.0 / QKD**0.5
    cache_scores = (
        jnp.einsum("rshk,rpk->rshp", query_steps, latent_cache, preferred_element_type=jnp.float32)
        * factor
    )
    fresh_scores = (
        jnp.einsum("rshk,rqk->rshq", query_steps, new_steps, preferred_element_type=jnp.float32)
        * factor
    )
    cache_live = (
        lax.broadcasted_iota(jnp.int32, cache_scores.shape, 3) < lengths[:, None, None, None]
    )
    fresh_live = lax.broadcasted_iota(jnp.int32, fresh_scores.shape, 3) <= lax.broadcasted_iota(
        jnp.int32, fresh_scores.shape, 1
    )
    cache_scores = jnp.where(cache_live, cache_scores, masked_score)
    fresh_scores = jnp.where(fresh_live, fresh_scores, masked_score)
    highest_score = jnp.maximum(jnp.max(cache_scores, axis=3), jnp.max(fresh_scores, axis=3))[
        ..., None
    ]
    cache_weight = jnp.where(cache_live, jnp.exp(cache_scores - highest_score), 0.0)
    fresh_weight = jnp.where(fresh_live, jnp.exp(fresh_scores - highest_score), 0.0)
    weight_sum = jnp.sum(cache_weight, axis=3) + jnp.sum(fresh_weight, axis=3)
    merged = jnp.einsum(
        "rshp,rpl->rshl",
        cache_weight.astype(jnp.bfloat16),
        latent_cache[:, :, :LAT],
        preferred_element_type=jnp.float32,
    )
    merged = merged + jnp.einsum(
        "rshq,rql->rshl",
        fresh_weight.astype(jnp.bfloat16),
        new_steps[:, :, :LAT],
        preferred_element_type=jnp.float32,
    )
    return (merged / weight_sum[..., None]).astype(jnp.bfloat16)


def local(
    queries,
    latent_cache,
    new_latent,
    lengths,
    residual,
    norm_gain,
    value_up,
    output_proj,
    expert_ids,
    expert_weights,
    gate_proj,
    up_proj,
    down_proj,
):
    requests = latent_cache.shape[0]
    positions = queries.shape[0] // requests
    head_count = queries.shape[1]
    feature = residual.shape[1]
    query_steps = queries.reshape(requests, positions, head_count, queries.shape[2])
    new_steps = new_latent.reshape(requests, positions, new_latent.shape[1])
    resid_steps = residual.reshape(requests, positions, feature)
    chosen_steps = expert_ids.reshape(requests, positions, expert_ids.shape[1])
    weight_steps = expert_weights.reshape(requests, positions, expert_weights.shape[1])
    expert_count = lax.axis_size("ep")
    side_count = lax.axis_size("side")
    full_rows = requests * positions
    capacity = min(
        full_rows, max(2, (full_rows * expert_ids.shape[1] + expert_count - 1) // expert_count)
    )
    uv_used, out_used = (
        lax.all_gather(value_up, "side", axis=0, tiled=True),
        lax.all_gather(output_proj, "side", axis=0, tiled=True),
    )
    flat_out = out_used.reshape(out_used.shape[0] * out_used.shape[1], feature)
    row_count = requests * positions
    latent = attend_block(query_steps, latent_cache, new_steps, lengths)
    latent = latent.reshape(row_count, head_count, latent.shape[3])
    arrived = lax.all_to_all(latent, "ep", split_axis=1, concat_axis=0, tiled=True)
    head_out = jnp.einsum(
        "ngl,glv->ngv", arrived, uv_used, preferred_element_type=jnp.float32
    ).astype(jnp.bfloat16)
    head_flat = head_out.reshape(head_out.shape[0], head_out.shape[1] * head_out.shape[2])
    attention = lax.psum_scatter(
        jnp.dot(head_flat, flat_out, preferred_element_type=jnp.float32),
        "ep",
        scatter_dimension=0,
        tiled=True,
    )
    resid_rows = resid_steps.reshape(row_count, feature)
    stream = resid_rows.astype(jnp.float32) + attention
    mean_square = jnp.mean(stream * stream, axis=1, keepdims=True)
    normed = (stream * lax.rsqrt(mean_square + norm_epsilon) * norm_gain[None, :]).astype(
        jnp.bfloat16
    )
    chosen_rows = chosen_steps.reshape(row_count, chosen_steps.shape[2])
    weight_rows = weight_steps.reshape(row_count, weight_steps.shape[2])
    chosen = chosen_rows[:, :, None] == lax.broadcasted_iota(jnp.int32, (1, 1, expert_count), 2)
    picked_count = jnp.sum(chosen.astype(jnp.int32), axis=1)
    routed_share = jnp.sum(jnp.where(chosen, weight_rows[:, :, None], 0.0), axis=1)
    before = jnp.cumsum(picked_count, axis=0) - picked_count
    placement = (before[:, :, None] == lax.broadcasted_iota(jnp.int32, (1, 1, capacity), 2)) & (
        picked_count[:, :, None] > 0
    )
    outbound = jnp.einsum(
        "nec,nd->ecd", placement.astype(jnp.bfloat16), normed, preferred_element_type=jnp.float32
    ).astype(jnp.bfloat16)
    outbound = jnp.broadcast_to(
        outbound[:, None], (expert_count, side_count, capacity, feature)
    ).reshape(expert_count * side_count, capacity, feature)
    arrived_rows = lax.all_to_all(outbound, ("ep", "side"), split_axis=0, concat_axis=0, tiled=True)
    source_total, item_total, width_total = arrived_rows.shape
    flat_rows = arrived_rows.reshape(source_total * item_total, width_total)
    gate_part = jnp.dot(flat_rows, gate_proj[0], preferred_element_type=jnp.float32)
    up_part = jnp.dot(flat_rows, up_proj[0], preferred_element_type=jnp.float32)
    hidden = (jax.nn.silu(gate_part) * up_part).astype(jnp.bfloat16)
    partial_value = jnp.dot(hidden, down_proj[0], preferred_element_type=jnp.float32).astype(
        jnp.bfloat16
    )
    partial_out = partial_value.reshape(source_total, item_total, width_total)
    returned = lax.all_to_all(partial_out, ("ep", "side"), split_axis=0, concat_axis=0, tiled=True)
    halves = returned.reshape(expert_count, side_count, capacity, feature).astype(jnp.float32)
    summed = jnp.sum(halves, axis=1)
    coefficient = jnp.where(placement, routed_share[:, :, None], 0.0)
    mixture = jnp.einsum("nec,ecd->nd", coefficient, summed, precision=lax.Precision.HIGHEST)
    output_rows = (stream + mixture).astype(jnp.bfloat16)
    output = output_rows.reshape(requests, positions, feature)
    return output.reshape(requests * positions, feature)


def solution(mesh):
    in_specs = (
        P(("groups", "ep", "side"), None, None),
        P(("groups", "ep", "side"), None, None),
        P(("groups", "ep", "side"), None),
        P(("groups", "ep", "side")),
        P(("groups", "ep", "side"), None),
        P(),
        P(("ep", "side"), None, None),
        P(("ep", "side"), None, None),
        P(("groups", "ep", "side"), None),
        P(("groups", "ep", "side"), None),
        P("ep", None, "side"),
        P("ep", None, "side"),
        P("ep", "side", None),
    )
    out_specs = P(("groups", "ep", "side"), None)
    return jax.shard_map(local, mesh=mesh, in_specs=in_specs, out_specs=out_specs, check_vma=False)
```

profile of v0, /device:TPU:0, one launch (start us, length us, event | category | flops | bytes accessed | tf_op | source)
XLA Modules:
  0.0 215.2 jit_solution(1367729353984791587)
XLA Ops:
  6.6 0.7 all-gather.3.cloned.1.call-update
  7.3 0.7 all-gather.5.cloned.1.call-update
  8.1 0.2 fusion.61
  8.4 0.3 fusion.60
  8.8 0.4 fusion.24
  9.3 0.4 fusion.8
  9.6 0.4 copy.35
  10.0 23.2 %all_to_all.28 = bf16[4,128,512]{2,0,1:T(4,128)(2,1)S(1)} all-to-all(bf16[4,128,512]{2,0,1:T(4,128)(2,1)S(1)} %copy.35), channel_id=1, replica_groups=mesh['groups'=1,'ep'=16,'side'=2] {'ep'}, dimensions={1} | all-to-all | bytes 1048576 | tf_op jit(solution)/shard_map/all_to_all | solution.py:91
  33.5 8.3 %all-gather.5.cloned.1.call-done = bf16[8,128,3584]{2,1,0:T(8,128)(2,1)} async-done(((bf16[4,128,3584]{2,1,0:T(8,128)(2,1)}), bf16[8,128,3584]{2,1,0:T(8,128)(2,1)}) %all-gather.5.cloned.1.call-update) | async-done | bytes 7340048 | tf_op jit(solution)/shard_map/all_gather | solution.py:85
  41.7 6.1 %convolution_bitcast_fusion = f32[64,3584]{1,0:T(8,128)} fusion(bf16[8,128,3584]{2,1,0:T(8,128)(2,1)} %all-gather.5.cloned.1.call-done, bf16[8,512,128]{2,1,0:T(8,128)(2,1)} %all-gather.3.cloned.1.call-done, bf16[64,8,512]{2,1,0:T(8,128)(2,1)S(1)} %bitcast.74), kind=kOutput, calls=%fused_computation | convolution fusion | flops 536936448 | bytes 9830400 | tf_op jit(solution)/shard_map/dot_general | solution.py:97
  48.0 0.6 dynamic-slice
  49.3 110.8 %all-reduce.3.cloned.1.call-done = f32[64,3584]{1,0:T(8,128)} async-done(((f32[64,3584]{1,0:T(8,128)}), f32[64,3584]{1,0:T(8,128)}) %all-reduce.3.cloned.1.call-update) | async-done | bytes 917520
  160.1 1.0 multiply_reduce_fusion
  161.1 1.2 convolution_convert_fusion.1
  162.3 0.2 copy.39
  162.6 0.2 broadcast_in_dim.60
  162.8 17.7 %all_to_all.29 = bf16[32,2,3584]{2,1,0:T(2,128)(2,1)S(1)} all-to-all(bf16[32,2,3584]{2,1,0:T(2,128)(2,1)S(1)} %bitcast.76), channel_id=1, replica_groups=mesh['groups'=1,'ep'=16,'side'=2] {'ep','side'}, dimensions={0} | all-to-all | bytes 917504 | tf_op jit(solution)/shard_map/all_to_all | solution.py:123
  180.7 2.8 %fusion.5 = f32[64,512]{1,0:T(8,128)S(1)} fusion(bf16[64,3584]{1,0:T(8,128)(2,1)S(1)} %reshape.64, bf16[1,3584,512]{2,1,0:T(8,128)(2,1)} %param.23), kind=kOutput, calls=%fused_computation.9 | convolution fusion | flops 234881024 | bytes 4259840 | tf_op jit(solution)/shard_map/dot_general | solution.py:126
  183.5 4.6 %convolution_convert_fusion = bf16[64,3584]{1,0:T(8,128)(2,1)S(1)} fusion(bf16[1,512,3584]{2,1,0:T(8,128)(2,1)} %param.25, bf16[64,3584]{1,0:T(8,128)(2,1)S(1)} %reshape.64, bf16[1,3584,512]{2,1,0:T(8,128)(2,1)} %param.24, f32[64,512]{1,0:T(8,128)S(1)} %fusion.5), kind=kOutput, calls=%fused_computation.1 | convolution fusion | flops 470188032 | bytes 8388608 | tf_op jit(solution)/shard_map/dot_general | solution.py:129
  188.1 0.9 reshape.65
  189.0 2.9 %all-to-all-start.2 = ((bf16[32,2,3584]{2,1,0:T(2,128)(2,1)}), bf16[32,2,3584]{2,1,0:T(2,128)(2,1)S(1)}, u32[]{:S(2)}, u32[]{:S(2)}) async-start(bf16[32,2,3584]{2,1,0:T(2,128)(2,1)} %reshape.65), calls=%async_computation.2 | async-start | bytes 917504 | tf_op jit(solution)/shard_map/all_to_all | solution.py:133
  192.0 14.3 %all-to-all-done.2 = bf16[32,2,3584]{2,1,0:T(2,128)(2,1)S(1)} async-done(((bf16[32,2,3584]{2,1,0:T(2,128)(2,1)}), bf16[32,2,3584]{2,1,0:T(2,128)(2,1)S(1)}, u32[]{:S(2)}, u32[]{:S(2)}) %all-to-all-start.2) | async-done | bytes 458784 | tf_op jit(solution)/shard_map/all_to_all | solution.py:133
  206.3 0.5 convert_reduce_fusion
  206.8 1.9 fusion.1
  (38 shorter events, 0.9 us)
Async XLA Ops:
  6.5 1.6 copy-start
  6.5 1.5 copy-start.3
  6.5 1.8 copy-start.1
  6.5 1.8 copy-start.6
  6.5 26.9 %all-gather.3.cloned.1.call-start = ((), (), s32[]{:S(2)}) async-start(), calls=%async_computation.3 | async-start | bytes 1572864 | tf_op jit(solution)/shard_map/all_gather | solution.py:84
  7.3 34.5 %all-gather.5.cloned.1.call-start = ((), (), s32[]{:S(2)}) async-start(), calls=%async_computation.4 | async-start | bytes 11010048 | tf_op jit(solution)/shard_map/all_gather | solution.py:85
  8.0 152.1 %all-reduce.3.cloned.1.call-start = ((), (), s32[]{:S(2)}) async-start(), calls=%async_computation.5 | async-start | bytes 1835008
  41.7 6.1 %copy-start.5 = (s32[4,8]{1,0:T(4,128)S(1)}, s32[4,8]{1,0:T(4,128)}, u32[]{:S(2)}) copy-start(s32[4,8]{1,0:T(4,128)} %param.21) | copy-start | bytes 388
  41.7 6.3 %copy-start.8 = (u32[32]{0:T(128)S(1)}, u32[32]{0:T(128)}, u32[]{:S(2)}) copy-start(u32[32]{0:T(128)} %constant.37) | copy-start | bytes 388
  41.7 118.3 %copy-start.2 = (bf16[4,3584]{1,0:T(4,128)(2,1)S(1)}, bf16[4,3584]{1,0:T(4,128)(2,1)}, u32[]{:S(2)}) copy-start(bf16[4,3584]{1,0:T(4,128)(2,1)} %param.17) | copy-start | bytes 86020
  41.7 119.4 %copy-start.4 = (f32[3584]{0:T(1024)S(1)}, f32[3584]{0:T(1024)}, u32[]{:S(2)}) copy-start(f32[3584]{0:T(1024)} %param.18) | copy-start | bytes 43012
  183.5 8.5 %copy-start.7 = (f32[4,8]{1,0:T(4,128)S(1)}, f32[4,8]{1,0:T(4,128)}, u32[]{:S(2)}) copy-start(f32[4,8]{1,0:T(4,128)} %param.22) | copy-start | bytes 388
  189.0 17.2 %all-to-all-start.2 = ((bf16[32,2,3584]{2,1,0:T(2,128)(2,1)}), bf16[32,2,3584]{2,1,0:T(2,128)(2,1)S(1)}, u32[]{:S(2)}, u32[]{:S(2)}) async-start(bf16[32,2,3584]{2,1,0:T(2,128)(2,1)} %reshape.65), calls=%async_computation.2 | async-start | bytes 917504 | tf_op jit(solution)/shard_map/all_to_all | solution.py:133
Sparse Core Ops, SparseCore 0:
  8.9 11.7 all-gather.2
  22.2 19.4 all-gather.4
  48.0 112.0 all-reduce.2
where the time goes:
time: 216 us; the launch traced here: 215 us
  waiting for transfers between devices  135 us (62%)
  blocking collectives  40.9 us (19%)
  matrix products  17.9 us (8%)
  between operations  14 us (6%)
  starting transfers between devices  2.97 us (1%)
  local copies, waits for them, and re-layouts  2.8 us (1%)
    unnamed x4, waiting for transfers between devices  112 us
    all_to_all x1, blocking collectives, local(): lax.all_to_all(latent, 'ep', split_axis=1, concat_axis=0, tiled=True)  23.2 us
    all_to_all x1, blocking collectives, local(): lax.all_to_all(outbound, ('ep', 'side'), split_axis=0, concat_axis=0, til...  17.7 us
    all_to_all x1, waiting for transfers between devices, local(): lax.all_to_all(partial_out, ('ep', 'side'), split_axis=0, concat_axis=0,...  14.3 us
    all_gather x1, waiting for transfers between devices, local(): lax.all_gather(output_proj, 'side', axis=0, tiled=True)  8.27 us
    dot_general x1, matrix products, local(): jnp.dot(head_flat, flat_out, preferred_element_type=jnp.float32)  6.09 us
    dot_general x1, matrix products, local(): jnp.dot(hidden, down_proj[0], preferred_element_type=jnp.float32)  4.62 us
  transfers between devices with their start and end apart: 4, of which 3 were waited for; matrix products, arithmetic and copies ran while one was open for 1% of the time, Pallas kernels for 0%

commit v1 on v0

v1 whole, which is shorter than its diff:
```python
import functools

import jax
import jax.numpy as jnp
import numpy as np
from jax import lax
from jax.experimental import pallas as pl
from jax.experimental.pallas import tpu as pltpu
from jax.sharding import PartitionSpec as P

LAT = 512
QKD = 192
MESH = pl.DeviceIdType.MESH
NORM_EPSILON = 1e-06
MASKED = -1e30
BF = jnp.bfloat16
F32 = jnp.float32


def remote(src, dst, send, recv, ep, side):
    return pltpu.make_async_remote_copy(
        src_ref=src,
        dst_ref=dst,
        send_sem=send,
        recv_sem=recv,
        device_id={"ep": ep, "side": side},
        device_id_type=MESH,
    )


def column_tile(width):
    return max(t for t in (512, 256, 128) if width % t == 0)


def kernel(
    dims,
    q_ref, cache_ref, fresh_ref, live_ref, fresh_live_ref, resid_ref, gain_ref, share_ref, pick_ref, head_ref,
    uv_hbm, op_hbm, gate_hbm, up_hbm, down_hbm,
    out_ref,
    uv, op, gate, up, down, weight_sem,
    lat_send, lat_recv, lat_ss, lat_rs,
    sh_recv, sh_ss, sh_rs, sh_rows,
    flat, hidden, acc, slab, blocks, stream, normed,
    s_send, s_recv, s_ss, s_rs,
    p_send, p_recv, p_ss, p_rs,
    z_send, z_recv, z_ss, z_rs,
    c1, c1_ss, c1_rs, xbuf, c2_ss, c2_rs, c3_ss, c3_rs,
):
    ep_n, sides, plane, zn, tok, hpd = dims
    n = ep_n * sides
    ep = lax.axis_index("ep")
    side = lax.axis_index("side")
    me = ep * sides + side
    z, c = ep // plane, ep % plane
    other = 1 - side
    my_slot = (side * plane + c) * zn + z
    feature = op_hbm.shape[2]
    quarters, piece = blocks.shape[1] // tok, blocks.shape[2]
    tile = column_tile(feature)

    barrier = pltpu.get_barrier_semaphore()

    @pl.loop(1, n)
    def _(k):
        d = (me + k) % n
        pl.semaphore_signal(
            barrier, inc=1, device_id={"ep": d // sides, "side": d % sides}, device_id_type=MESH
        )

    loads = [
        pltpu.make_async_copy(uv_hbm, uv, weight_sem.at[0]),
        pltpu.make_async_copy(op_hbm.at[0], op, weight_sem.at[1]),
        pltpu.make_async_copy(gate_hbm.at[0], gate, weight_sem.at[2]),
        pltpu.make_async_copy(up_hbm.at[0], up, weight_sem.at[3]),
        pltpu.make_async_copy(down_hbm.at[0], down, weight_sem.at[4]),
    ]
    for load in loads:
        load.start()

    factor = 1.0 / QKD**0.5
    merged_all = []
    for r in range(q_ref.shape[0]):
        q, keys, fresh = q_ref[r], cache_ref[r], fresh_ref[r]
        dims_t = (((1,), (1,)), ((), ()))
        s1 = lax.dot_general(q, keys, dims_t, preferred_element_type=F32) * factor
        s2 = lax.dot_general(q, fresh, dims_t, preferred_element_type=F32) * factor
        live1 = live_ref[r] > 0.0
        live2 = fresh_live_ref[...] > 0.0
        s1 = jnp.where(live1, s1, MASKED)
        s2 = jnp.where(live2, s2, MASKED)
        top = jnp.maximum(
            jnp.max(s1, axis=1, keepdims=True), jnp.max(s2, axis=1, keepdims=True)
        )
        w1 = jnp.where(live1, jnp.exp(s1 - top), 0.0)
        w2 = jnp.where(live2, jnp.exp(s2 - top), 0.0)
        total = jnp.sum(w1, axis=1, keepdims=True) + jnp.sum(w2, axis=1, keepdims=True)
        merged = jnp.dot(w1.astype(BF), keys[:, :LAT], preferred_element_type=F32)
        merged = merged + jnp.dot(w2.astype(BF), fresh[:, :LAT], preferred_element_type=F32)
        merged = merged / total
        merged_all.append(merged.reshape(n, merged.shape[0] // n, LAT))
    lat_send[...] = jnp.concatenate(merged_all, axis=1).astype(BF)

    pl.semaphore_wait(barrier, n - 1)

    def lat_copy(d, slot):
        return remote(
            lat_send.at[d], lat_recv.at[slot], lat_ss.at[d], lat_rs.at[slot], d // sides, d % sides
        )

    def share_copy(d, slot):
        return remote(
            share_ref, sh_recv.at[slot], sh_ss.at[d], sh_rs.at[slot], d // sides, d % sides
        )

    @pl.loop(1, n)
    def _(k):
        d = (me + k) % n
        lat_copy(d, me).start()

    @pl.loop(1, n)
    def _(k):
        d = (me + k) % n
        share_copy(d, my_slot).start()

    lat_recv[me] = lat_send[me]
    sh_recv[my_slot] = share_ref[...]
    loads[0].wait()
    loads[1].wait()

    @pl.loop(1, n)
    def _(k):
        d = (me + k) % n
        lat_copy(d, d).wait_recv()

    arrived = lat_recv[...].reshape(lat_recv.shape[0] * lat_recv.shape[1], LAT)
    width = uv.shape[2]
    for h in range(hpd):
        raised = jnp.dot(arrived, uv[h], preferred_element_type=F32).astype(BF)
        for half in range(2):
            picked = jnp.dot(pick_ref[half] * head_ref[h], raised, preferred_element_type=F32)
            flat[half, :, h * width : (h + 1) * width] = picked.astype(BF)

    def scatter_sum(g, value):
        @pl.loop(0, feature // tile)
        def _(j):
            cols = pl.ds(pl.multiple_of(j * tile, tile), tile)
            part = value(other, cols)
            s_send[g, :, :, cols] = part.reshape(plane, zn * tok, tile).astype(BF)

        pair = remote(s_send.at[g], s_recv.at[g], s_ss.at[g], s_rs.at[g], ep, other)
        pair.start()

        @pl.loop(0, feature // tile)
        def _(j):
            cols = pl.ds(pl.multiple_of(j * tile, tile), tile)
            acc[:, :, cols] = value(side, cols).reshape(plane, zn * tok, tile)

        pair.wait_recv()

        def plane_copy(k, slot):
            peer = (c + k) % plane
            return remote(
                p_send.at[g, peer], p_recv.at[g, slot], p_ss.at[g, peer], p_rs.at[g, slot],
                z * plane + peer, side,
            )

        @pl.loop(1, plane)
        def _(k):
            peer = (c + k) % plane
            p_send[g, peer] = (acc[peer] + s_recv[g, peer].astype(F32)).astype(BF)
            plane_copy(k, c).start()

        slab[...] = acc[c] + s_recv[g, c].astype(F32)

        @pl.loop(1, plane)
        def _(k):
            peer = (c + k) % plane
            plane_copy(k, peer).wait_recv()
            slab[...] += p_recv[g, peer].astype(F32)

        for layer in range(zn):
            for a in range(quarters):
                blocks[layer, a * tok : (a + 1) * tok, :] = slab[
                    layer * tok : (layer + 1) * tok, a * piece : (a + 1) * piece
                ]
        z_send[g] = blocks[...].astype(BF)

        def z_copy(k, slot):
            peer = (z + k) % zn
            return remote(
                z_send.at[g, peer], z_recv.at[g, slot], z_ss.at[g, peer], z_rs.at[g, slot],
                peer * plane + c, side,
            )

        for k in range(1, zn):
            z_copy(k, z).start()
        result = blocks[z]
        for k in range(1, zn):
            peer = (z + k) % zn
            z_copy(k, peer).wait_recv()
            result = result + z_recv[g, peer].astype(F32)

        def finish():
            pair.wait_send()

            @pl.loop(1, plane)
            def _(k):
                plane_copy(k, c).wait_send()

            for k in range(1, zn):
                z_copy(k, z).wait_send()

        return result, finish

    def attention_part(half, cols):
        return jnp.dot(flat[half], op[:, cols], preferred_element_type=F32)

    attention, finish_attention = scatter_sum(0, attention_part)
    stream[...] = resid_ref[...] + attention

    square = jnp.zeros((tok, 1), F32)
    for a in range(quarters):
        rows = stream[a * tok : (a + 1) * tok, :]
        square = square + jnp.sum(rows * rows, axis=1, keepdims=True)
    scale = lax.rsqrt(square * (1.0 / feature) + NORM_EPSILON)
    for a in range(quarters):
        normed[a * tok : (a + 1) * tok, :] = (
            stream[a * tok : (a + 1) * tok, :] * scale * gain_ref[a * tok : (a + 1) * tok, :]
        )
    c1[z] = normed[...].astype(BF)

    def line_copy(k, slot):
        peer = (z + k) % zn
        return remote(
            c1.at[z], c1.at[slot], c1_ss.at[peer], c1_rs.at[slot], peer * plane + c, side
        )

    for k in range(1, zn):
        line_copy(k, z).start()

    @pl.loop(1, n)
    def _(k):
        d = (me + k) % n
        e, s = d // sides, d % sides
        share_copy(d, (s * plane + e % plane) * zn + e // plane).wait_recv()

    for slot in range(n):
        sh_rows[slot * tok : (slot + 1) * tok, :] = sh_recv[slot, :tok, :]
    lanes = lax.broadcasted_iota(jnp.int32, sh_rows.shape, 1)
    share = jnp.sum(jnp.where(lanes == ep, sh_rows[...], 0.0), axis=1, keepdims=True)
    sh_rows[...] = jnp.broadcast_to(share, sh_rows.shape)

    for k in range(1, zn):
        peer = (z + k) % zn
        line_copy(k, peer).wait_recv()
    for layer in range(zn):
        blocks[layer] = c1[layer].astype(F32)
    for layer in range(zn):
        for a in range(quarters):
            slab[layer * tok : (layer + 1) * tok, a * piece : (a + 1) * piece] = blocks[
                layer, a * tok : (a + 1) * tok, :
            ]
    xbuf[side, c] = slab[...].astype(BF)

    def spread_copy(k, slot):
        peer = (c + k) % plane
        return remote(
            xbuf.at[side, c], xbuf.at[side, slot], c2_ss.at[peer], c2_rs.at[slot],
            z * plane + peer, side,
        )

    def pair_copy(slot, half):
        return remote(
            xbuf.at[half, slot], xbuf.at[half, slot], c3_ss.at[slot], c3_rs.at[slot], ep, other
        )

    @pl.loop(1, plane)
    def _(k):
        spread_copy(k, c).start()

    pair_copy(c, side).start()

    @pl.loop(1, plane)
    def _(k):
        peer = (c + k) % plane
        spread_copy(k, peer).wait_recv()
        pair_copy(peer, side).start()

    loads[2].wait()
    loads[3].wait()
    loads[4].wait()
    half_rows = plane * zn * tok

    def hidden_half(half):
        rows = xbuf[half].reshape(half_rows, feature)
        units = gate.shape[1]
        step = min(units, 256)
        for j in range(units // step):
            cols = slice(j * step, (j + 1) * step)
            gated = jnp.dot(rows, gate[:, cols], preferred_element_type=F32)
            raised = jnp.dot(rows, up[:, cols], preferred_element_type=F32)
            hidden[half, :, cols] = (gated / (1.0 + jnp.exp(-gated)) * raised).astype(BF)

    hidden_half(side)

    @pl.loop(0, plane)
    def _(k):
        pair_copy(k, other).wait_recv()

    hidden_half(other)

    def expert_part(half, cols):
        part = jnp.dot(hidden[half], down[:, cols], preferred_element_type=F32)
        rows = pl.ds(pl.multiple_of(half * half_rows, half_rows), half_rows)
        return part.astype(BF).astype(F32) * sh_rows[rows, :1]

    mixture, finish_mixture = scatter_sum(1, expert_part)
    out_ref[...] = (stream[...] + mixture).astype(BF)

    finish_attention()
    finish_mixture()

    @pl.loop(1, n)
    def _(k):
        d = (me + k) % n
        lat_copy(d, me).wait_send()
        share_copy(d, my_slot).wait_send()

    for k in range(1, zn):
        line_copy(k, z).wait_send()

    @pl.loop(1, plane)
    def _(k):
        spread_copy(k, c).wait_send()

    @pl.loop(0, plane)
    def _(k):
        pair_copy(k, side).wait_send()


def local(
    queries, latent_cache, new_latent, lengths, residual, norm_gain, value_up, output_proj,
    expert_ids, expert_weights, gate_proj, up_proj, down_proj,
):
    ep_n, sides = lax.axis_size("ep"), lax.axis_size("side")
    n = ep_n * sides
    requests, context, key_width = latent_cache.shape
    tok, head_count, _ = queries.shape
    steps = tok // requests
    hpd = value_up.shape[0]
    feature = residual.shape[1]
    plane = 1
    while plane * plane < ep_n:
        plane *= 2
    zn = ep_n // plane
    quarters = 16 // tok
    piece = feature // quarters
    rq = -(-steps * hpd // 8) * 8
    fresh_rows = 16

    q = queries.reshape(requests, steps, n, hpd, key_width).transpose(0, 2, 1, 3, 4)
    q = q.reshape(requests, n, steps * hpd, key_width)
    q = jnp.pad(q, ((0, 0), (0, 0), (0, rq - steps * hpd), (0, 0)))
    q = q.reshape(requests, n * rq, key_width)
    fresh = new_latent.reshape(requests, steps, key_width)
    fresh = jnp.pad(fresh, ((0, 0), (0, fresh_rows - steps), (0, 0)))
    live = (
        lax.broadcasted_iota(jnp.int32, (requests, 1, context), 2) < lengths[:, None, None]
    ).astype(F32)
    own_step = np.minimum((np.arange(n * rq) % rq) // hpd, steps - 1)
    fresh_live = (np.arange(fresh_rows)[None, :] <= own_step[:, None]).astype(np.float32)

    lat_rows = requests * rq
    pick = np.zeros((n, tok, n, lat_rows), np.float32)
    heads = np.zeros((hpd, n, lat_rows), np.float32)
    for d in range(n):
        e, s = d // sides, d % sides
        slot = (s * plane + e % plane) * zn + e // plane
        for t in range(tok):
            first = (t // steps) * rq + (t % steps) * hpd
            pick[slot, t, d, first : first + hpd] = 1.0
    for r in range(requests):
        for j in range(steps):
            for h in range(hpd):
                heads[h, :, r * rq + j * hpd + h] = 1.0
    pick = jnp.asarray(pick.reshape(sides, n * tok // sides, n * lat_rows), BF)
    heads = jnp.asarray(heads.reshape(hpd, 1, n * lat_rows), BF)

    def blocked(rows):
        return rows.reshape(tok, quarters, piece).transpose(1, 0, 2).reshape(quarters * tok, piece)

    resid = blocked(residual.astype(F32))
    gain = blocked(jnp.broadcast_to(norm_gain[None, :], (tok, feature)))
    lanes = -(-ep_n // 128) * 128
    chosen = expert_ids[:, :, None] == lax.broadcasted_iota(jnp.int32, (1, 1, lanes), 2)
    share = jnp.sum(jnp.where(chosen, expert_weights[:, :, None], 0.0), axis=1)
    share = jnp.pad(share, ((0, 8 - tok), (0, 0)))

    op = output_proj.reshape(1, hpd * output_proj.shape[1], feature)
    values = value_up.shape[2]
    units = gate_proj.shape[2]
    half = n * tok // 2
    zr = zn * tok
    blk = quarters * tok
    dma, vm = pltpu.SemaphoreType.DMA, pltpu.VMEM
    scratch = [
        vm(value_up.shape, BF), vm((hpd * values, feature), BF),
        vm((feature, units), BF), vm((feature, units), BF), vm((units, feature), BF), dma((5,)),
        vm((n, lat_rows, LAT), BF), vm((n, lat_rows, LAT), BF), dma((n,)), dma((n,)),
        vm((n, 8, lanes), F32), dma((n,)), dma((n,)), vm((n * tok, lanes), F32),
        vm((2, half, hpd * values), BF), vm((2, half, units), BF), vm((plane, zr, feature), F32),
        vm((zr, feature), F32), vm((zn, blk, piece), F32), vm((blk, piece), F32), vm((blk, piece), F32),
        vm((2, plane, zr, feature), BF), vm((2, plane, zr, feature), BF), dma((2,)), dma((2,)),
        vm((2, plane, zr, feature), BF), vm((2, plane, zr, feature), BF), dma((2, plane)), dma((2, plane)),
        vm((2, zn, blk, piece), BF), vm((2, zn, blk, piece), BF), dma((2, zn)), dma((2, zn)),
        vm((zn, blk, piece), BF), dma((zn,)), dma((zn,)),
        vm((2, plane, zr, feature), BF), dma((plane,)), dma((plane,)), dma((plane,)), dma((plane,)),
    ]
    in_vmem = pl.BlockSpec(memory_space=pltpu.VMEM)
    in_hbm = pl.BlockSpec(memory_space=pl.ANY)

    body = functools.partial(kernel, (ep_n, sides, plane, zn, tok, hpd))
    out = pl.pallas_call(
        body,
        out_shape=jax.ShapeDtypeStruct((blk, piece), BF),
        in_specs=[in_vmem] * 10 + [in_hbm] * 5,
        out_specs=in_vmem,
        scratch_shapes=scratch,
        compiler_params=pltpu.CompilerParams(
            collective_id=0, has_side_effects=True, vmem_limit_bytes=60 * 2**20
        ),
    )(
        q, latent_cache, fresh, live, jnp.asarray(fresh_live), resid, gain, share, pick, heads,
        value_up, op, gate_proj, up_proj, down_proj,
    )
    return out.reshape(quarters, tok, piece).transpose(1, 0, 2).reshape(tok, feature)


def solution(mesh):
    rows = ("groups", "ep", "side")
    in_specs = (
        P(rows, None, None),
        P(rows, None, None),
        P(rows, None),
        P(rows),
        P(rows, None),
        P(),
        P(("ep", "side"), None, None),
        P(("ep", "side"), None, None),
        P(rows, None),
        P(rows, None),
        P("ep", None, "side"),
        P("ep", None, "side"),
        P("ep", "side", None),
    )
    return jax.shard_map(
        local, mesh=mesh, in_specs=in_specs, out_specs=P(rows, None), check_vma=False
    )
```

time: 216 us -> 79.1 us (0.37)
  waiting for transfers between devices: 135 us -> 0 us
  Pallas kernels: 0 us -> 70 us
  blocking collectives: 40.9 us -> 0 us
  matrix products: 17.9 us -> 0 us
  between operations: 14 us -> 0.07 us
  local copies, waits for them, and re-layouts: 2.8 us -> 8.01 us
  starting transfers between devices: 2.97 us -> 0 us
    unnamed x4 -> x0, waiting for transfers between devices: 112 us -> none
    pallas_call x0 -> x1, Pallas kernels: none -> 70 us  [local(): pl.pallas_call(body, out_shape=jax.ShapeDtypeStruct((blk, piece), BF), in...]
    all_to_all x2 -> x0, blocking collectives: 40.9 us -> none  [the longest x1 23.2 us: local(): lax.all_to_all(latent, 'ep', split_axis=1, concat_axis=0, tiled=True)]
    dot_general x9 -> x0, matrix products: 17.9 us -> none  [the longest x1 6.09 us: local(): jnp.dot(head_flat, flat_out, preferred_element_type=jnp.float32)]
    all_to_all x1 -> x0, waiting for transfers between devices: 14.3 us -> none  [local(): lax.all_to_all(partial_out, ('ep', 'side'), split_axis=0, concat_axis=0,...]
    all_gather x2 -> x0, waiting for transfers between devices: 8.29 us -> none  [the longest x1 8.27 us: local(): lax.all_gather(output_proj, 'side', axis=0, tiled=True)]
    all_to_all x1 -> x0, starting transfers between devices: 2.86 us -> none  [local(): lax.all_to_all(partial_out, ('ep', 'side'), split_axis=0, concat_axis=0,...]
    reshape x5 -> x6, local copies, waits for them, and re-layouts: 1.57 us -> 3.77 us  [the longest x1 1.37 us: local(): out.reshape(quarters, tok, piece).transpose(1, 0, 2).reshape(tok, feature)]
  transfers between devices with their start and end apart: 4 -> 0, of which waited for: 3 -> 0; matrix products, arithmetic and copies ran while one was open for 1% -> 0% of each run, Pallas kernels for 0% -> 0%
where the time goes in v1:
time: 79.1 us; the launch traced here: 78.9 us
  Pallas kernels  70 us (88%)
  local copies, waits for them, and re-layouts  8.01 us (10%)
    pallas_call x1, Pallas kernels, local(): pl.pallas_call(body, out_shape=jax.ShapeDtypeStruct((blk, piece), BF), in...  70 us
    unnamed x16, local copies, waits for them, and re-layouts  2.33 us

profile of v1, /device:TPU:0, one launch (start us, length us, event | category | flops | bytes accessed | tf_op | source)
XLA Modules:
  0.0 78.9 jit_solution(11570272784297132475)
XLA Ops:
  0.0 0.0 copy-start.2
  0.0 0.0 copy-start.1
  0.0 0.0 copy-start.4
  0.0 0.0 copy-start.6
  0.0 1.4 %copy.27 = bf16[4,128,576]{2,1,0:T(8,128)(2,1)S(1)} copy(bf16[4,128,576]{1,2,0:T(8,128)(2,1)} %param.16) | data formatting | bytes 1179648 | tf_op args[0]
  1.4 0.2 reshape.73
  1.6 0.7 copy.28
  2.3 0.9 %copy.30.q_ref = bf16[2,256,576]{2,1,0:T(8,128)(2,1)} copy(bf16[2,256,576]{2,0,1:T(2,128)(2,1)S(1)} %bitcast.12) | data formatting | bytes 1179648 | tf_op jit(solution)/shard_map/reshape | solution.py:364
  3.2 0.0 copy-done
  3.2 0.9 %copy.31.cache_ref = bf16[2,128,576]{2,1,0:T(8,128)(2,1)} copy(bf16[2,128,576]{1,2,0:T(8,128)(2,1)S(1)} %copy-done) | data formatting | bytes 589824 | tf_op args[1]
  4.1 0.0 copy-done.2
  4.2 0.6 reshape.79.gain_ref
  4.8 0.0 copy-done.1
  4.8 0.7 reshape.84.resid_ref
  5.5 0.0 copy-done.3
  5.5 0.6 pad.8.fresh_ref
  6.1 0.0 copy-done.5
  6.1 0.0 copy-done.4
  6.1 0.1 select_reduce_fusion
  6.2 0.6 pad.9.share_ref
  6.8 0.0 copy-done.6
  6.8 0.7 compare_convert_fusion.live_ref
  7.5 70.0 %shard_map.154 = bf16[16,896]{1,0:T(8,128)(2,1)} custom-call(bf16[2,256,576]{2,1,0:T(8,128)(2,1)} %copy.30.q_ref, bf16[2,128,576]{2,1,0:T(8,128)(2,1)} %copy.31.cache_ref, bf16[2,16,576]{2,1,0:T(8,128)(2,1)} %pad.8.fresh_ref, f32[2,1,128]{2,1,0:T(1,128)} %compare_convert_fusion.live_ref, f32[256,16]{1,0:T(8,128)} %constant.14.clone.fresh_live_ref, ...), custom_call_target="tpu_custom_call" | custom-call | tf_op jit(solution)/shard_map/pallas_call | solution.py:423
  77.5 1.4 %reshape.81 = bf16[4,4,896]{2,1,0:T(4,128)(2,1)} reshape(bf16[16,896]{1,0:T(8,128)(2,1)} %shard_map.154) | data formatting | bytes 57344 | tf_op jit(solution)/shard_map/reshape | solution.py:436
  (7 shorter events, 0.1 us)
Async XLA Ops:
  0.0 3.2 %copy-start = (bf16[2,128,576]{1,2,0:T(8,128)(2,1)S(1)}, bf16[2,128,576]{1,2,0:T(8,128)(2,1)}, u32[]{:S(2)}) copy-start(bf16[2,128,576]{1,2,0:T(8,128)(2,1)} %param.17) | copy-start | bytes 884740
  0.0 4.1 %copy-start.2 = (f32[3584]{0:T(1024)S(1)}, f32[3584]{0:T(1024)}, u32[]{:S(2)}) copy-start(f32[3584]{0:T(1024)} %param.21) | copy-start | bytes 43012
  0.0 4.8 %copy-start.1 = (bf16[4,3584]{1,0:T(4,128)(2,1)S(1)}, bf16[4,3584]{1,0:T(4,128)(2,1)}, u32[]{:S(2)}) copy-start(bf16[4,3584]{1,0:T(4,128)(2,1)} %param.20) | copy-start | bytes 86020
  0.0 5.5 %copy-start.3 = (bf16[4,576]{1,0:T(4,128)(2,1)S(1)}, bf16[4,576]{1,0:T(4,128)(2,1)}, u32[]{:S(2)}) copy-start(bf16[4,576]{1,0:T(4,128)(2,1)} %param.18) | copy-start | bytes 13828
  0.0 6.1 %copy-start.5 = (s32[4,8]{1,0:T(4,128)S(1)}, s32[4,8]{1,0:T(4,128)}, u32[]{:S(2)}) copy-start(s32[4,8]{1,0:T(4,128)} %param.24) | copy-start | bytes 388
  0.0 6.1 %copy-start.4 = (f32[4,8]{1,0:T(4,128)S(1)}, f32[4,8]{1,0:T(4,128)}, u32[]{:S(2)}) copy-start(f32[4,8]{1,0:T(4,128)} %param.25) | copy-start | bytes 388
  0.0 6.8 %copy-start.6 = (s32[2]{0:T(128)S(1)}, s32[2]{0:T(128)}, u32[]{:S(2)}) copy-start(s32[2]{0:T(128)} %param.19) | copy-start | bytes 28

commit v2 on v1

v2 whole, which is shorter than its diff:
```python
import functools

import jax
import jax.numpy as jnp
import numpy as np
from jax import lax
from jax.experimental import pallas as pl
from jax.experimental.pallas import tpu as pltpu
from jax.sharding import PartitionSpec as P

LAT = 512
QKD = 192
MESH = pl.DeviceIdType.MESH
NORM_EPSILON = 1e-06
MASKED = -1e30
BF = jnp.bfloat16
F32 = jnp.float32


def remote(src, dst, send, recv, ep, side):
    return pltpu.make_async_remote_copy(
        src_ref=src,
        dst_ref=dst,
        send_sem=send,
        recv_sem=recv,
        device_id={"ep": ep, "side": side},
        device_id_type=MESH,
    )


def kernel(
    dims,
    q_ref, cache_ref, fresh_ref, lengths_ref, resid_ref, gain_ref, ids_ref, weights_ref,
    fresh_live_ref, perm_ref, pick_ref, head_ref, sel_ref,
    uv_hbm, op_hbm, gate_hbm, up_hbm, down_hbm,
    out_ref,
    uv, op, gate, up, down, weight_sem,
    fresh_rows, lat_send, lat_recv, lat_ss, lat_rs, raised,
    sh_send, sh_recv, sh_ss, sh_rs, sh_rows,
    flat, hidden, acc, slab, blocks, total, stream, gains, squares, rows_out,
    s_send, s_recv, s_ss, s_rs,
    p_send, p_recv, p_ss, p_rs,
    z_send, z_recv, z_ss, z_rs,
    xblk, xrows, l_ss, l_rs, c_ss, c_rs, x_ss, x_rs,
):
    ep_n, sides, plane, zn, tok, hpd = dims
    n = ep_n * sides
    ep = lax.axis_index("ep")
    side = lax.axis_index("side")
    me = ep * sides + side
    z, c = ep // plane, ep % plane
    other = 1 - side
    my_slot = (side * plane + c) * zn + z
    feature = op_hbm.shape[2]
    chunks, quarters, piece = total.shape[0], total.shape[1] // tok, total.shape[2]
    tile = quarters * piece
    values = uv_hbm.shape[2]

    barrier = pltpu.get_barrier_semaphore()

    @pl.loop(1, n)
    def _(k):
        d = (me + k) % n
        pl.semaphore_signal(
            barrier, inc=1, device_id={"ep": d // sides, "side": d % sides}, device_id_type=MESH
        )

    loads = [
        pltpu.make_async_copy(uv_hbm.at[h], uv.at[:, pl.ds(h * values, values)], weight_sem.at[h])
        for h in range(hpd)
    ] + [
        pltpu.make_async_copy(op_hbm.at[0], op, weight_sem.at[hpd]),
        pltpu.make_async_copy(gate_hbm.at[0], gate, weight_sem.at[hpd + 1]),
        pltpu.make_async_copy(up_hbm.at[0], up, weight_sem.at[hpd + 2]),
        pltpu.make_async_copy(down_hbm.at[0], down, weight_sem.at[hpd + 3]),
    ]
    for load in loads:
        load.start()

    factor = 1.0 / QKD**0.5
    requests = cache_ref.shape[0]
    steps = tok // requests
    fresh_rows[...] = jnp.zeros_like(fresh_rows)
    fresh_rows[:tok, :] = fresh_ref[...].astype(F32)
    fresh = fresh_rows[...].astype(BF)
    merged_all = []
    for r in range(requests):
        q = jnp.concatenate([q_ref[r * steps + j].T for j in range(steps)], axis=0)
        keys = cache_ref[r]
        dims_t = (((1,), (1,)), ((), ()))
        s1 = jnp.dot(q, keys, preferred_element_type=F32) * factor
        s2 = lax.dot_general(q, fresh, dims_t, preferred_element_type=F32) * factor
        live1 = lax.broadcasted_iota(jnp.int32, s1.shape, 1) < lengths_ref[r]
        live2 = fresh_live_ref[r] > 0.0
        s1 = jnp.where(live1, s1, MASKED)
        s2 = jnp.where(live2, s2, MASKED)
        top = jnp.maximum(
            jnp.max(s1, axis=1, keepdims=True), jnp.max(s2, axis=1, keepdims=True)
        )
        w1 = jnp.where(live1, jnp.exp(s1 - top), 0.0)
        w2 = jnp.where(live2, jnp.exp(s2 - top), 0.0)
        weight_sum = jnp.sum(w1, axis=1, keepdims=True) + jnp.sum(w2, axis=1, keepdims=True)
        merged = lax.dot_general(
            w1.astype(BF), keys[:LAT, :], dims_t, preferred_element_type=F32
        )
        merged = merged + jnp.dot(w2.astype(BF), fresh[:, :LAT], preferred_element_type=F32)
        merged = (merged / weight_sum).astype(BF)
        ordered = jnp.dot(perm_ref[...].astype(BF), merged, preferred_element_type=F32)
        merged_all.append(ordered.reshape(n, ordered.shape[0] // n, LAT))
    lat_send[...] = jnp.concatenate(merged_all, axis=1).astype(BF)

    pl.semaphore_wait(barrier, n - 1)

    def lat_copy(d, slot):
        return remote(
            lat_send.at[d], lat_recv.at[slot], lat_ss.at[d], lat_rs.at[slot], d // sides, d % sides
        )

    def share_copy(d, slot):
        return remote(
            sh_send, sh_recv.at[slot], sh_ss.at[d], sh_rs.at[slot], d // sides, d % sides
        )

    @pl.loop(1, n)
    def _(k):
        lat_copy((me + (k * 13) % n) % n, me).start()

    lanes = lax.broadcasted_iota(jnp.int32, (tok, sh_send.shape[1]), 1)
    shares = jnp.zeros((tok, sh_send.shape[1]), F32)
    for k in range(ids_ref.shape[1]):
        shares = shares + jnp.where(
            lanes == ids_ref[:, k : k + 1], weights_ref[:, k : k + 1], 0.0
        )
    sh_send[...] = jnp.zeros_like(sh_send)
    sh_send[:tok, :] = shares

    @pl.loop(1, n)
    def _(k):
        share_copy((me + k) % n, my_slot).start()

    lat_recv[me] = lat_send[me]
    sh_recv[my_slot] = sh_send[...]

    rows_out[...] = resid_ref[...].astype(F32)
    for j in range(chunks):
        for a in range(quarters):
            cols = slice(j * tile + a * piece, j * tile + (a + 1) * piece)
            stream[j, a * tok : (a + 1) * tok, :] = rows_out[:, cols]
            gains[j, a * tok : (a + 1) * tok, :] = jnp.broadcast_to(gain_ref[:, cols], (tok, piece))

    for load in loads[: hpd + 1]:
        load.wait()

    group = plane * sides
    lat_rows = lat_recv.shape[1]

    @pl.loop(0, zn)
    def _(k):
        layer = (z + k) % zn

        @pl.loop(0, group)
        def _(i):
            d = layer * group + i

            @pl.when(d != me)
            def _():
                lat_copy(d, d).wait_recv()

        arrived = lat_recv[pl.ds(layer * group, group)].reshape(group * lat_rows, LAT)
        up_rows = jnp.dot(arrived, uv[...], preferred_element_type=F32).astype(BF)
        raised[layer] = up_rows * head_ref[...].astype(BF)

    everyone = raised[...].reshape(zn * group * lat_rows, raised.shape[2])
    for half in range(2):
        flat[half] = jnp.dot(pick_ref[half].astype(BF), everyone, preferred_element_type=F32).astype(BF)

    def scatter_sum(g, value):
        def pair(j):
            return remote(s_send.at[g, j], s_recv.at[g, j], s_ss.at[g, j], s_rs.at[g, j], ep, other)

        def plane_copy(j, k, slot):
            peer = (c + k) % plane
            return remote(
                p_send.at[g, j, peer], p_recv.at[g, j, slot], p_ss.at[g, j, peer],
                p_rs.at[g, j, slot], z * plane + peer, side,
            )

        def z_copy(j, k, slot):
            peer = (z + k) % zn
            return remote(
                z_send.at[g, j, peer], z_recv.at[g, j, slot], z_ss.at[g, j, peer],
                z_rs.at[g, j, slot], peer * plane + c, side,
            )

        def produce(j):
            cols = pl.ds(pl.multiple_of(j * tile, tile), tile)
            s_send[g, j] = value(other, cols).reshape(plane, zn * tok, tile).astype(BF)
            pair(j).start()
            acc[j] = value(side, cols).reshape(plane, zn * tok, tile)

        def spread(j):
            pair(j).wait_recv()
            for k in range(1, plane):
                peer = (c + k) % plane
                p_send[g, j, peer] = (acc[j, peer] + s_recv[g, j, peer].astype(F32)).astype(BF)
                plane_copy(j, k, c).start()

        produce(0)

        @pl.loop(1, chunks)
        def _(j):
            produce(j)
            spread(j - 1)

        spread(chunks - 1)

        @pl.loop(0, chunks)
        def _(j):
            own = acc[j, c] + s_recv[g, j, c].astype(F32)
            for k in range(1, plane):
                peer = (c + k) % plane
                plane_copy(j, k, peer).wait_recv()
                own = own + p_recv[g, j, peer].astype(F32)
            slab[...] = own
            for layer in range(zn):
                for a in range(quarters):
                    blocks[layer, a * tok : (a + 1) * tok, :] = slab[
                        layer * tok : (layer + 1) * tok, a * piece : (a + 1) * piece
                    ]
            z_send[g, j] = blocks[...].astype(BF)
            total[j] = blocks[z]
            for k in range(1, zn):
                z_copy(j, k, z).start()

        @pl.loop(0, chunks)
        def _(j):
            result = total[j]
            for k in range(1, zn):
                peer = (z + k) % zn
                z_copy(j, k, peer).wait_recv()
                result = result + z_recv[g, j, peer].astype(F32)
            total[j] = result

        def finish():
            @pl.loop(0, chunks)
            def _(j):
                pair(j).wait_send()
                for k in range(1, plane):
                    plane_copy(j, k, c).wait_send()
                for k in range(1, zn):
                    z_copy(j, k, z).wait_send()

        return finish

    def attention_part(half, cols):
        return jnp.dot(flat[half], op[:, cols], preferred_element_type=F32)

    finish_attention = scatter_sum(0, attention_part)
    stream[...] = stream[...] + total[...]

    square = jnp.sum(jnp.sum(stream[...] * stream[...], axis=0), axis=1, keepdims=True)
    squares[...] = jnp.broadcast_to(square, squares.shape)
    token_square = squares[:tok, :]
    for a in range(1, quarters):
        token_square = token_square + squares[a * tok : (a + 1) * tok, :]
    scale = lax.rsqrt(token_square * (1.0 / feature) + NORM_EPSILON)
    for a in range(quarters):
        squares[a * tok : (a + 1) * tok, :] = scale
    for j in range(chunks):
        xblk[side, c, z, :, j * piece : (j + 1) * piece] = (
            stream[j] * squares[...] * gains[j]
        ).astype(BF)

    def line_copy(k, slot):
        peer = (z + k) % zn
        return remote(
            xblk.at[side, c, z], xblk.at[side, c, slot], l_ss.at[peer], l_rs.at[slot],
            peer * plane + c, side,
        )

    def plane_rows(k, slot, layer):
        peer = (c + k) % plane
        return remote(
            xblk.at[side, c, layer], xblk.at[side, slot, layer], c_ss.at[peer, layer],
            c_rs.at[slot, layer], z * plane + peer, side,
        )

    def pair_rows(slot, layer, half):
        return remote(
            xblk.at[half, slot, layer], xblk.at[half, slot, layer], x_ss.at[slot, layer],
            x_rs.at[slot, layer], ep, other,
        )

    def hand_on(layer):
        for k in range(1, plane):
            plane_rows(k, c, layer).start()
        pair_rows(c, layer, side).start()

    for k in range(1, zn):
        line_copy(k, z).start()
    hand_on(z)

    @pl.loop(1, n)
    def _(k):
        d = (me + k) % n
        e, s = d // sides, d % sides
        share_copy(d, (s * plane + e % plane) * zn + e // plane).wait_recv()

    for slot in range(n):
        sh_rows[slot * tok : (slot + 1) * tok, :] = sh_recv[slot, :tok, :]
    all_lanes = lax.broadcasted_iota(jnp.int32, sh_rows.shape, 1)
    share = jnp.sum(jnp.where(all_lanes == ep, sh_rows[...], 0.0), axis=1, keepdims=True)
    sh_rows[...] = jnp.broadcast_to(share, sh_rows.shape)

    @pl.loop(0, zn)
    def _(kz):
        layer = (z + kz) % zn

        @pl.when(kz + 1 < zn)
        def _():
            line_copy(kz + 1, (z + kz + 1) % zn).wait_recv()
            hand_on((z + kz + 1) % zn)

        for k in range(1, plane):
            peer = (c + k) % plane
            plane_rows(k, peer, layer).wait_recv()
            pair_rows(peer, layer, side).start()

    for load in loads[hpd + 1 :]:
        load.wait()
    half_rows = plane * zn * tok

    def hidden_half(half):
        travelled = xblk[half].reshape(half_rows * quarters, chunks * piece)
        for a in range(quarters):
            rows = jnp.dot(sel_ref[a].astype(BF), travelled, preferred_element_type=F32).astype(BF)
            for j in range(chunks):
                first = j * tile + a * piece
                xrows[:, first : first + piece] = rows[:, j * piece : (j + 1) * piece]
        units = gate.shape[1]
        step = min(units, 256)
        for j in range(units // step):
            cols = slice(j * step, (j + 1) * step)
            gated = jnp.dot(xrows[...], gate[:, cols], preferred_element_type=F32)
            lifted = jnp.dot(xrows[...], up[:, cols], preferred_element_type=F32)
            hidden[half, :, cols] = (gated / (1.0 + jnp.exp(-gated)) * lifted).astype(BF)

    hidden_half(side)

    @pl.loop(0, plane)
    def _(k):
        @pl.loop(0, zn)
        def _(layer):
            pair_rows(k, layer, other).wait_recv()

    hidden_half(other)

    def expert_part(half, cols):
        part = jnp.dot(hidden[half], down[:, cols], preferred_element_type=F32)
        rows = pl.ds(pl.multiple_of(half * half_rows, half_rows), half_rows)
        return part.astype(BF).astype(F32) * sh_rows[rows, :1]

    finish_mixture = scatter_sum(1, expert_part)
    stream[...] = stream[...] + total[...]
    for j in range(chunks):
        for a in range(quarters):
            cols = slice(j * tile + a * piece, j * tile + (a + 1) * piece)
            rows_out[:, cols] = stream[j, a * tok : (a + 1) * tok, :]
    out_ref[...] = rows_out[...].astype(BF)

    finish_attention()
    finish_mixture()

    @pl.loop(1, n)
    def _(k):
        d = (me + k) % n
        lat_copy(d, me).wait_send()
        share_copy(d, my_slot).wait_send()

    for k in range(1, zn):
        line_copy(k, z).wait_send()

    @pl.loop(0, zn)
    def _(layer):
        for k in range(1, plane):
            plane_rows(k, c, layer).wait_send()

        @pl.loop(0, plane)
        def _(slot):
            pair_rows(slot, layer, side).wait_send()


def local(
    queries, latent_cache, new_latent, lengths, residual, norm_gain, value_up, output_proj,
    expert_ids, expert_weights, gate_proj, up_proj, down_proj,
):
    ep_n, sides = lax.axis_size("ep"), lax.axis_size("side")
    n = ep_n * sides
    requests, context, key_width = latent_cache.shape
    tok, head_count, _ = queries.shape
    steps = tok // requests
    hpd = value_up.shape[0]
    feature = residual.shape[1]
    plane = 1
    while plane * plane < ep_n:
        plane *= 2
    zn = ep_n // plane
    quarters = 16 // tok
    piece = 128
    tile = quarters * piece
    chunks = feature // tile
    rq = -(-steps * hpd // 8) * 8
    fresh_count = 16
    lat_rows = requests * rq
    values = value_up.shape[2]
    units = gate_proj.shape[2]

    key = np.arange(fresh_count)[None, None, :]
    request = np.arange(requests)[:, None, None]
    step = (np.arange(steps * head_count) // head_count)[None, :, None]
    fresh_live = (key // steps == request) & (key % steps <= step) & (key < tok)

    perm = np.zeros((n, rq, steps * head_count), np.float32)
    for d in range(n):
        for j in range(steps):
            for h in range(hpd):
                perm[d, j * hpd + h, j * head_count + d * hpd + h] = 1.0
    perm = perm.reshape(n * rq, steps * head_count)

    pick = np.zeros((n, tok, n, lat_rows), np.float32)
    heads = np.zeros((plane * sides, lat_rows, hpd, values), np.float32)
    for d in range(n):
        e, s = d // sides, d % sides
        slot = (s * plane + e % plane) * zn + e // plane
        for t in range(tok):
            first = (t // steps) * rq + (t % steps) * hpd
            pick[slot, t, d, first : first + hpd] = 1.0
    for t in range(tok):
        for h in range(hpd):
            heads[:, (t // steps) * rq + (t % steps) * hpd + h, h] = 1.0
    pick = pick.reshape(sides, n * tok // sides, n * lat_rows)
    heads = heads.reshape(plane * sides * lat_rows, hpd * values)

    slots = ep_n
    sel = np.zeros((quarters, slots, tok, slots, quarters, tok), np.float32)
    for a in range(quarters):
        for slot in range(slots):
            for t in range(tok):
                sel[a, slot, t, slot, a, t] = 1.0
    sel = sel.reshape(quarters, slots * tok, slots * quarters * tok)

    lanes = -(-ep_n // 128) * 128
    op = output_proj.reshape(1, hpd * output_proj.shape[1], feature)
    half = n * tok // 2
    zr = zn * tok
    blk = quarters * tok
    dma, vm = pltpu.SemaphoreType.DMA, pltpu.VMEM
    scratch = [
        vm((LAT, hpd * values), BF), vm((hpd * values, feature), BF),
        vm((feature, units), BF), vm((feature, units), BF), vm((units, feature), BF), dma((hpd + 4,)),
        vm((fresh_count, key_width), F32),
        vm((n, lat_rows, LAT), BF), vm((n, lat_rows, LAT), BF), dma((n,)), dma((n,)),
        vm((zn, plane * sides * lat_rows, hpd * values), BF),
        vm((8, lanes), F32), vm((n, 8, lanes), F32), dma((n,)), dma((n,)), vm((n * tok, lanes), F32),
        vm((2, half, hpd * values), BF), vm((2, half, units), BF),
        vm((chunks, plane, zr, tile), F32), vm((zr, tile), F32), vm((zn, blk, piece), F32),
        vm((chunks, blk, piece), F32), vm((chunks, blk, piece), F32), vm((chunks, blk, piece), F32),
        vm((blk, piece), F32), vm((tok, feature), F32),
        vm((2, chunks, plane, zr, tile), BF), vm((2, chunks, plane, zr, tile), BF),
        dma((2, chunks)), dma((2, chunks)),
        vm((2, chunks, plane, zr, tile), BF), vm((2, chunks, plane, zr, tile), BF),
        dma((2, chunks, plane)), dma((2, chunks, plane)),
        vm((2, chunks, zn, blk, piece), BF), vm((2, chunks, zn, blk, piece), BF),
        dma((2, chunks, zn)), dma((2, chunks, zn)),
        vm((sides, plane, zn, blk, chunks * piece), BF), vm((half, feature), BF),
        dma((zn,)), dma((zn,)), dma((plane, zn)), dma((plane, zn)), dma((plane, zn)), dma((plane, zn)),
    ]
    in_vmem = pl.BlockSpec(memory_space=pltpu.VMEM)
    in_smem = pl.BlockSpec(memory_space=pltpu.SMEM)
    in_hbm = pl.BlockSpec(memory_space=pl.ANY)
    body = functools.partial(kernel, (ep_n, sides, plane, zn, tok, hpd))
    return pl.pallas_call(
        body,
        out_shape=jax.ShapeDtypeStruct((tok, feature), BF),
        in_specs=[in_vmem] * 3 + [in_smem] + [in_vmem] * 9 + [in_hbm] * 5,
        out_specs=in_vmem,
        scratch_shapes=scratch,
        compiler_params=pltpu.CompilerParams(
            collective_id=0, has_side_effects=True, vmem_limit_bytes=60 * 2**20
        ),
    )(
        queries.transpose(0, 2, 1), latent_cache.transpose(0, 2, 1), new_latent, lengths, residual,
        norm_gain.reshape(1, feature),
        expert_ids, expert_weights, jnp.asarray(fresh_live, F32), jnp.asarray(perm),
        jnp.asarray(pick), jnp.asarray(heads), jnp.asarray(sel),
        value_up, op, gate_proj, up_proj, down_proj,
    )


def solution(mesh):
    rows = ("groups", "ep", "side")
    in_specs = (
        P(rows, None, None),
        P(rows, None, None),
        P(rows, None),
        P(rows),
        P(rows, None),
        P(),
        P(("ep", "side"), None, None),
        P(("ep", "side"), None, None),
        P(rows, None),
        P(rows, None),
        P("ep", None, "side"),
        P("ep", None, "side"),
        P("ep", "side", None),
    )
    return jax.shard_map(
        local, mesh=mesh, in_specs=in_specs, out_specs=P(rows, None), check_vma=False
    )
```

time: 79.1 us -> 73.2 us (0.925)
  local copies, waits for them, and re-layouts: 8.01 us -> 2.69 us
    reshape x6 -> x1, local copies, waits for them, and re-layouts: 3.77 us -> 1.33 us  [local(): norm_gain.reshape(1, feature)]
    pad x2 -> x0, local copies, waits for them, and re-layouts: 1.22 us -> none  [the longest x1 0.62 us: local(): fresh = jnp.pad(fresh, ((0, 0), (0, fresh_rows - steps), (0, 0)))]
    unnamed x16 -> x1, local copies, waits for them, and re-layouts: 2.33 us -> 1.37 us
where the time goes in v2:
time: 73.2 us; the launch traced here: 73 us
  Pallas kernels  70.3 us (96%)
  local copies, waits for them, and re-layouts  2.69 us (4%)
    pallas_call x1, Pallas kernels, local(): pl.pallas_call(body, out_shape=jax.ShapeDtypeStruct((tok, feature), BF),...  70.3 us

profile of v2, /device:TPU:0, one launch (start us, length us, event | category | flops | bytes accessed | tf_op | source)
XLA Modules:
  0.0 73.0 jit_solution(17311120359682126394)
XLA Ops:
  0.0 1.3 %reshape.6.gain_ref = f32[1,3584]{1,0:T(1,128)} reshape(f32[3584]{0:T(1024)} %param.23) | data formatting | bytes 28672 | tf_op jit(solution)/shard_map/reshape | solution.py:493
  1.3 70.3 %shard_map.172 = bf16[4,3584]{1,0:T(4,128)(2,1)} custom-call(bf16[4,576,128]{2,1,0:T(8,128)(2,1)} %bitcast.4, bf16[2,576,128]{2,1,0:T(8,128)(2,1)} %bitcast.5, bf16[4,576]{1,0:T(4,128)(2,1)} %fresh_ref.1, s32[2]{0:T(128)} %lengths_ref.1, bf16[4,3584]{1,0:T(4,128)(2,1)} %resid_ref.1, f32[1,3584]{1,0:T(1,128)} %reshape.6.gain_ref, s32[4,8]{1,0:T(4,128)} %ids_ref.1, ...), custom_call_target="tpu_custom_call" | custom-call | tf_op jit(solution)/shard_map/pallas_call | solution.py:482
  71.6 1.4 %copy.20 = bf16[4,3584]{1,0:T(4,128)(2,1)} copy(bf16[4,3584]{1,0:T(4,128)(2,1)} %shard_map.172) | data formatting | bytes 57344

commit v3 on v2

v3 whole, which is shorter than its diff:
```python
import functools

import jax
import jax.numpy as jnp
import numpy as np
from jax import lax
from jax.experimental import pallas as pl
from jax.experimental.pallas import tpu as pltpu
from jax.sharding import PartitionSpec as P

LAT = 512
QKD = 192
MESH = pl.DeviceIdType.MESH
NORM_EPSILON = 1e-06
MASKED = -1e30
BF = jnp.bfloat16
F32 = jnp.float32


def remote(src, dst, send, recv, ep, side):
    return pltpu.make_async_remote_copy(
        src_ref=src,
        dst_ref=dst,
        send_sem=send,
        recv_sem=recv,
        device_id={"ep": ep, "side": side},
        device_id_type=MESH,
    )


def kernel(
    dims,
    q_ref, cache_ref, fresh_ref, lengths_ref, resid_ref, gain_ref, ids_ref, weights_ref,
    fresh_live_ref, perm_ref, pick_ref, head_ref, sel_ref,
    uv_hbm, op_hbm, gate_hbm, up_hbm, down_hbm,
    out_ref,
    uv, op, gate, up, down, weight_sem,
    fresh_rows, lat_send, lat_recv, lat_ss, lat_rs, raised,
    shares, sh_rows,
    flat, hidden, acc, slab, blocks, total, stream, gains, squares, rows_out,
    s_send, s_recv, s_ss, s_rs,
    p_send, p_recv, p_ss, p_rs,
    z_send, z_recv, z_ss, z_rs,
    xblk, xrows, l_ss, l_rs, c_ss, c_rs, x_ss, x_rs,
):
    ep_n, sides, plane, zn, tok, hpd = dims
    n = ep_n * sides
    ep = lax.axis_index("ep")
    side = lax.axis_index("side")
    me = ep * sides + side
    z, c = ep // plane, ep % plane
    other = 1 - side
    feature = op_hbm.shape[2]
    chunks, quarters, piece = total.shape[0], total.shape[1] // tok, total.shape[2]
    tile = quarters * piece
    values = uv_hbm.shape[2]

    barrier = pltpu.get_barrier_semaphore()

    @pl.loop(1, n)
    def _(k):
        d = (me + k) % n
        pl.semaphore_signal(
            barrier, inc=1, device_id={"ep": d // sides, "side": d % sides}, device_id_type=MESH
        )

    loads = [
        pltpu.make_async_copy(uv_hbm.at[h], uv.at[:, pl.ds(h * values, values)], weight_sem.at[h])
        for h in range(hpd)
    ] + [
        pltpu.make_async_copy(op_hbm.at[0], op, weight_sem.at[hpd]),
        pltpu.make_async_copy(gate_hbm.at[0], gate, weight_sem.at[hpd + 1]),
        pltpu.make_async_copy(up_hbm.at[0], up, weight_sem.at[hpd + 2]),
        pltpu.make_async_copy(down_hbm.at[0], down, weight_sem.at[hpd + 3]),
    ]
    for load in loads:
        load.start()

    factor = 1.0 / QKD**0.5
    requests = cache_ref.shape[0]
    steps = tok // requests
    fresh_rows[...] = jnp.zeros_like(fresh_rows)
    fresh_rows[:tok, :] = fresh_ref[...].astype(F32)
    fresh = fresh_rows[...].astype(BF)
    merged_all = []
    for r in range(requests):
        q = jnp.concatenate([q_ref[r * steps + j].T for j in range(steps)], axis=0)
        keys = cache_ref[r]
        dims_t = (((1,), (1,)), ((), ()))
        s1 = jnp.dot(q, keys, preferred_element_type=F32) * factor
        s2 = lax.dot_general(q, fresh, dims_t, preferred_element_type=F32) * factor
        live1 = lax.broadcasted_iota(jnp.int32, s1.shape, 1) < lengths_ref[r]
        live2 = fresh_live_ref[r] > 0.0
        s1 = jnp.where(live1, s1, MASKED)
        s2 = jnp.where(live2, s2, MASKED)
        top = jnp.maximum(
            jnp.max(s1, axis=1, keepdims=True), jnp.max(s2, axis=1, keepdims=True)
        )
        w1 = jnp.where(live1, jnp.exp(s1 - top), 0.0)
        w2 = jnp.where(live2, jnp.exp(s2 - top), 0.0)
        weight_sum = jnp.sum(w1, axis=1, keepdims=True) + jnp.sum(w2, axis=1, keepdims=True)
        merged = lax.dot_general(
            w1.astype(BF), keys[:LAT, :], dims_t, preferred_element_type=F32
        )
        merged = merged + jnp.dot(w2.astype(BF), fresh[:, :LAT], preferred_element_type=F32)
        merged = (merged / weight_sum).astype(BF)
        ordered = jnp.dot(perm_ref[...].astype(BF), merged, preferred_element_type=F32)
        merged_all.append(ordered.reshape(n, ordered.shape[0] // n, LAT))
    lat_send[...] = jnp.concatenate(merged_all, axis=1).astype(BF)

    pl.semaphore_wait(barrier, n - 1)

    def lat_copy(d, slot):
        return remote(
            lat_send.at[d], lat_recv.at[slot], lat_ss, lat_rs.at[z], d // sides, d % sides
        )

    @pl.loop(1, n)
    def _(k):
        lat_copy((me + (k * 13) % n) % n, me).start()

    lat_recv[me] = lat_send[me]

    lanes = lax.broadcasted_iota(jnp.int32, (tok, shares.shape[1]), 1)
    share = jnp.zeros((tok, shares.shape[1]), F32)
    for k in range(ids_ref.shape[1]):
        share = share + jnp.where(lanes == ids_ref[:, k : k + 1], weights_ref[:, k : k + 1], 0.0)
    shares[...] = jnp.zeros_like(shares)
    for a in range(3):
        term = share.astype(BF).astype(F32)
        shares[a * tok : (a + 1) * tok, :] = term
        share = share - term
    xblk[side, z, c, :, chunks * piece :] = shares[...].astype(BF)

    rows_out[...] = resid_ref[...].astype(F32)
    for j in range(chunks):
        for a in range(quarters):
            cols = slice(j * tile + a * piece, j * tile + (a + 1) * piece)
            stream[j, a * tok : (a + 1) * tok, :] = rows_out[:, cols]
            gains[j, a * tok : (a + 1) * tok, :] = jnp.broadcast_to(
                gain_ref[cols][None, :], (tok, piece)
            )

    for load in loads[: hpd + 1]:
        load.wait()

    group = plane * sides
    lat_rows = lat_recv.shape[1]

    for k in range(zn):
        layer = (z + k) % zn
        got = lat_recv.at[pl.ds(layer * group, group if k else group - 1)]
        remote(got, got, lat_ss, lat_rs.at[layer], ep, other).wait_recv()
        arrived = lat_recv[pl.ds(layer * group, group)].reshape(group * lat_rows, LAT)
        up_rows = jnp.dot(arrived, uv[...], preferred_element_type=F32).astype(BF)
        raised[layer] = up_rows * head_ref[...].astype(BF)

    everyone = raised[...].reshape(zn * group * lat_rows, raised.shape[2])
    flat[...] = jnp.dot(pick_ref[...].astype(BF), everyone, preferred_element_type=F32).astype(BF)

    cut = -(-chunks // 2)
    groups = ((0, cut), (cut, chunks - cut))

    def scatter_sum(g, value):
        def pair(i):
            part = pl.ds(*groups[i])
            return remote(
                s_send.at[g, part], s_recv.at[g, part], s_ss.at[g, i], s_rs.at[g, i], ep, other
            )

        def plane_copy(i, k):
            peer, part = (c + k) % plane, pl.ds(*groups[i])
            return remote(
                p_send.at[g, peer, part], p_recv.at[g, c, part], p_ss.at[g, i], p_rs.at[g, i],
                z * plane + peer, side,
            )

        def z_copy(i, k):
            peer, part = (z + k) % zn, pl.ds(*groups[i])
            return remote(
                z_send.at[g, peer, part], z_recv.at[g, z, part], z_ss.at[g, i], z_rs.at[g, i],
                peer * plane + c, side,
            )

        def all_plane(i):
            some, part = pl.ds(0, plane - 1), pl.ds(*groups[i])
            return remote(
                p_send.at[g, some, part], p_recv.at[g, some, part], p_ss.at[g, i], p_rs.at[g, i],
                ep, other,
            )

        def all_z(i):
            some, part = pl.ds(0, zn - 1), pl.ds(*groups[i])
            return remote(
                z_send.at[g, some, part], z_recv.at[g, some, part], z_ss.at[g, i], z_rs.at[g, i],
                ep, other,
            )

        def chunk_loop(i):
            return pl.loop(groups[i][0], groups[i][0] + groups[i][1])

        for i in range(2):

            @chunk_loop(i)
            def _(j):
                cols = pl.ds(pl.multiple_of(j * tile, tile), tile)
                acc[j] = value(cols).reshape(sides, plane, zn * tok, tile)
                s_send[g, j] = acc[j, other].astype(BF)

            pair(i).start()

        for i in range(2):
            pair(i).wait_recv()
            for k in range(1, plane):
                peer = (c + k) % plane

                @chunk_loop(i)
                def _(j):
                    p_send[g, peer, j] = (
                        acc[j, side, peer] + s_recv[g, j, peer].astype(F32)
                    ).astype(BF)

                plane_copy(i, k).start()

        for i in range(2):
            all_plane(i).wait_recv()

            @chunk_loop(i)
            def _(j):
                own = acc[j, side, c] + s_recv[g, j, c].astype(F32)
                for k in range(1, plane):
                    own = own + p_recv[g, (c + k) % plane, j].astype(F32)
                slab[...] = own
                for layer in range(zn):
                    for a in range(quarters):
                        blocks[layer, a * tok : (a + 1) * tok, :] = slab[
                            layer * tok : (layer + 1) * tok, a * piece : (a + 1) * piece
                        ]
                for layer in range(zn):
                    z_send[g, layer, j] = blocks[layer].astype(BF)
                total[j] = blocks[z]

            for k in range(1, zn):
                z_copy(i, k).start()

        for i in range(2):
            all_z(i).wait_recv()

            @chunk_loop(i)
            def _(j):
                result = total[j]
                for k in range(1, zn):
                    result = result + z_recv[g, (z + k) % zn, j].astype(F32)
                total[j] = result

        def finish():
            for i in range(2):
                pair(i).wait_send()
                all_plane(i).wait_send()
                all_z(i).wait_send()

        return finish

    def attention_part(cols):
        return jnp.dot(flat[...], op[:, cols], preferred_element_type=F32)

    finish_attention = scatter_sum(0, attention_part)
    stream[...] = stream[...] + total[...]

    square = jnp.sum(jnp.sum(stream[...] * stream[...], axis=0), axis=1, keepdims=True)
    squares[...] = jnp.broadcast_to(square, squares.shape)
    token_square = squares[:tok, :]
    for a in range(1, quarters):
        token_square = token_square + squares[a * tok : (a + 1) * tok, :]
    scale = lax.rsqrt(token_square * (1.0 / feature) + NORM_EPSILON)
    for a in range(quarters):
        squares[a * tok : (a + 1) * tok, :] = scale
    for j in range(chunks):
        xblk[side, z, c, :, j * piece : (j + 1) * piece] = (
            stream[j] * squares[...] * gains[j]
        ).astype(BF)

    def line_copy(k, slot):
        peer = (z + k) % zn
        return remote(
            xblk.at[side, z, c], xblk.at[side, slot, c], l_ss.at[peer], l_rs.at[slot],
            peer * plane + c, side,
        )

    def plane_rows(k, layer):
        return remote(
            xblk.at[side, layer, c], xblk.at[side, layer, c], c_ss.at[layer], c_rs.at[layer],
            z * plane + (c + k) % plane, side,
        )

    def plane_all(layer):
        some = xblk.at[side, layer, pl.ds(0, plane - 1)]
        return remote(some, some, c_ss.at[layer], c_rs.at[layer], ep, other)

    def pair_rows(layer, half):
        return remote(
            xblk.at[half, layer], xblk.at[half, layer], x_ss.at[layer], x_rs.at[layer], ep, other
        )

    for k in range(1, zn):
        line_copy(k, z).start()
    for k in range(1, plane):
        plane_rows(k, z).start()
    for kz in range(zn):
        layer, following = (z + kz) % zn, (z + kz + 1) % zn
        if kz + 1 < zn:
            line_copy(kz + 1, following).wait_recv()
            for k in range(1, plane):
                plane_rows(k, following).start()
        plane_all(layer).wait_recv()
        pair_rows(layer, side).start()

    for load in loads[hpd + 1 :]:
        load.wait()
    half_rows = plane * zn * tok

    def unpack(half):
        travelled = xblk[half].reshape(half_rows * quarters, xblk.shape[4])
        rows = jnp.dot(sel_ref[...].astype(BF), travelled, preferred_element_type=F32)
        for a in range(quarters):
            for j in range(chunks):
                first = j * tile + a * piece
                xrows[half, :, first : first + piece] = rows[
                    a * half_rows : (a + 1) * half_rows, j * piece : (j + 1) * piece
                ].astype(BF)
        terms = rows[:half_rows, chunks * piece :]
        for a in range(1, 3):
            terms = terms + rows[a * half_rows : (a + 1) * half_rows, chunks * piece :]
        which = lax.broadcasted_iota(jnp.int32, terms.shape, 1)
        weight = jnp.sum(jnp.where(which == ep, terms, 0.0), axis=1, keepdims=True)
        sh_rows[half] = jnp.broadcast_to(weight, sh_rows.shape[1:])

    unpack(side)
    for layer in range(zn):
        pair_rows(layer, other).wait_recv()
    unpack(other)

    units = gate.shape[1]
    step = min(units, 256)
    everything = xrows[...].reshape(sides * half_rows, feature)
    for j in range(units // step):
        cols = slice(j * step, (j + 1) * step)
        gated = jnp.dot(everything, gate[:, cols], preferred_element_type=F32)
        lifted = jnp.dot(everything, up[:, cols], preferred_element_type=F32)
        hidden[:, cols] = (gated / (1.0 + jnp.exp(-gated)) * lifted).astype(BF)

    def expert_part(cols):
        part = jnp.dot(hidden[...], down[:, cols], preferred_element_type=F32)
        weight = sh_rows[...].reshape(sides * half_rows, sh_rows.shape[2])[:, :1]
        return part.astype(BF).astype(F32) * weight

    finish_mixture = scatter_sum(1, expert_part)
    stream[...] = stream[...] + total[...]
    for j in range(chunks):
        for a in range(quarters):
            cols = slice(j * tile + a * piece, j * tile + (a + 1) * piece)
            rows_out[:, cols] = stream[j, a * tok : (a + 1) * tok, :]
    out_ref[...] = rows_out[...].astype(BF)

    finish_attention()
    finish_mixture()
    sent = lat_send.at[pl.ds(0, n - 1)]
    remote(sent, sent, lat_ss, lat_rs.at[0], ep, other).wait_send()
    for k in range(1, zn):
        line_copy(k, z).wait_send()
    for layer in range(zn):
        plane_all(layer).wait_send()
        pair_rows(layer, side).wait_send()


def local(
    queries, latent_cache, new_latent, lengths, residual, norm_gain, value_up, output_proj,
    expert_ids, expert_weights, gate_proj, up_proj, down_proj,
):
    ep_n, sides = lax.axis_size("ep"), lax.axis_size("side")
    n = ep_n * sides
    requests, context, key_width = latent_cache.shape
    tok, head_count, _ = queries.shape
    steps = tok // requests
    hpd = value_up.shape[0]
    feature = residual.shape[1]
    plane = 1
    while plane * plane < ep_n:
        plane *= 2
    zn = ep_n // plane
    quarters = 16 // tok
    piece = 128
    tile = quarters * piece
    chunks = feature // tile
    rq = -(-steps * hpd // 8) * 8
    fresh_count = 16
    lat_rows = requests * rq
    values = value_up.shape[2]
    units = gate_proj.shape[2]

    key = np.arange(fresh_count)[None, None, :]
    request = np.arange(requests)[:, None, None]
    step = (np.arange(steps * head_count) // head_count)[None, :, None]
    fresh_live = (key // steps == request) & (key % steps <= step) & (key < tok)

    perm = np.zeros((n, rq, steps * head_count), np.float32)
    for d in range(n):
        for j in range(steps):
            for h in range(hpd):
                perm[d, j * hpd + h, j * head_count + d * hpd + h] = 1.0
    perm = perm.reshape(n * rq, steps * head_count)

    pick = np.zeros((n, tok, n, lat_rows), np.float32)
    heads = np.zeros((plane * sides, lat_rows, hpd, values), np.float32)
    for d in range(n):
        e, s = d // sides, d % sides
        slot = (s * plane + e % plane) * zn + e // plane
        for t in range(tok):
            first = (t // steps) * rq + (t % steps) * hpd
            pick[slot, t, d, first : first + hpd] = 1.0
    for t in range(tok):
        for h in range(hpd):
            heads[:, (t // steps) * rq + (t % steps) * hpd + h, h] = 1.0
    pick = pick.reshape(n * tok, n * lat_rows)
    heads = heads.reshape(plane * sides * lat_rows, hpd * values)

    sel = np.zeros((quarters, plane, zn, tok, zn, plane, quarters, tok), np.float32)
    for a in range(quarters):
        for e in range(ep_n):
            for t in range(tok):
                sel[a, e % plane, e // plane, t, e // plane, e % plane, a, t] = 1.0
    sel = sel.reshape(quarters * ep_n * tok, ep_n * quarters * tok)

    lanes = -(-ep_n // 128) * 128
    op = output_proj.reshape(1, hpd * output_proj.shape[1], feature)
    half = n * tok // 2
    zr = zn * tok
    blk = quarters * tok
    dma, vm = pltpu.SemaphoreType.DMA, pltpu.VMEM
    scratch = [
        vm((LAT, hpd * values), BF), vm((hpd * values, feature), BF),
        vm((feature, units), BF), vm((feature, units), BF), vm((units, feature), BF), dma((hpd + 4,)),
        vm((fresh_count, key_width), F32),
        vm((n, lat_rows, LAT), BF), vm((n, lat_rows, LAT), BF), dma(()), dma((zn,)),
        vm((zn, plane * sides * lat_rows, hpd * values), BF),
        vm((blk, lanes), F32), vm((sides, half, lanes), F32),
        vm((2 * half, hpd * values), BF), vm((2 * half, units), BF),
        vm((chunks, sides, plane, zr, tile), F32), vm((zr, tile), F32), vm((zn, blk, piece), F32),
        vm((chunks, blk, piece), F32), vm((chunks, blk, piece), F32), vm((chunks, blk, piece), F32),
        vm((blk, piece), F32), vm((tok, feature), F32),
        vm((2, chunks, plane, zr, tile), BF), vm((2, chunks, plane, zr, tile), BF),
        dma((2, 2)), dma((2, 2)),
        vm((2, plane, chunks, zr, tile), BF), vm((2, plane, chunks, zr, tile), BF),
        dma((2, 2)), dma((2, 2)),
        vm((2, zn, chunks, blk, piece), BF), vm((2, zn, chunks, blk, piece), BF),
        dma((2, 2)), dma((2, 2)),
        vm((sides, zn, plane, blk, chunks * piece + lanes), BF), vm((sides, half, feature), BF),
        dma((zn,)), dma((zn,)), dma((zn,)), dma((zn,)), dma((zn,)), dma((zn,)),
    ]
    in_vmem = pl.BlockSpec(memory_space=pltpu.VMEM)
    in_smem = pl.BlockSpec(memory_space=pltpu.SMEM)
    in_hbm = pl.BlockSpec(memory_space=pl.ANY)
    body = functools.partial(kernel, (ep_n, sides, plane, zn, tok, hpd))
    return pl.pallas_call(
        body,
        out_shape=jax.ShapeDtypeStruct((tok, feature), BF),
        in_specs=[in_vmem] * 3 + [in_smem] + [in_vmem] * 9 + [in_hbm] * 5,
        out_specs=in_vmem,
        scratch_shapes=scratch,
        compiler_params=pltpu.CompilerParams(
            collective_id=0, has_side_effects=True, vmem_limit_bytes=60 * 2**20
        ),
    )(
        queries.transpose(0, 2, 1), latent_cache.transpose(0, 2, 1), new_latent, lengths, residual,
        norm_gain,
        expert_ids, expert_weights, jnp.asarray(fresh_live, F32), jnp.asarray(perm),
        jnp.asarray(pick), jnp.asarray(heads), jnp.asarray(sel),
        value_up, op, gate_proj, up_proj, down_proj,
    )


def solution(mesh):
    rows = ("groups", "ep", "side")
    in_specs = (
        P(rows, None, None),
        P(rows, None, None),
        P(rows, None),
        P(rows),
        P(rows, None),
        P(),
        P(("ep", "side"), None, None),
        P(("ep", "side"), None, None),
        P(rows, None),
        P(rows, None),
        P("ep", None, "side"),
        P("ep", None, "side"),
        P("ep", "side", None),
    )
    return jax.shard_map(
        local, mesh=mesh, in_specs=in_specs, out_specs=P(rows, None), check_vma=False
    )
```

time: 73.2 us -> 65.9 us (0.900)
  Pallas kernels: 70.3 us -> 64.3 us
  local copies, waits for them, and re-layouts: 2.69 us -> 1.37 us
    pallas_call x1, Pallas kernels: 70.3 us -> 64.3 us  [local(): pl.pallas_call(body, out_shape=jax.ShapeDtypeStruct((tok, feature), BF),...]
    reshape x1 -> x0, local copies, waits for them, and re-layouts: 1.33 us -> none  [local(): norm_gain.reshape(1, feature)]
where the time goes in v3:
time: 65.9 us; the launch traced here: 65.7 us
  Pallas kernels  64.3 us (98%)
  local copies, waits for them, and re-layouts  1.37 us (2%)
    pallas_call x1, Pallas kernels, local(): pl.pallas_call(body, out_shape=jax.ShapeDtypeStruct((tok, feature), BF),...  64.3 us
    unnamed x1, local copies, waits for them, and re-layouts  1.37 us

profile of v3, /device:TPU:0, one launch (start us, length us, event | category | flops | bytes accessed | tf_op | source)
XLA Modules:
  0.0 65.7 jit_solution(5837983111881246969)
XLA Ops:
  0.0 64.3 %shard_map.172 = bf16[4,3584]{1,0:T(4,128)(2,1)} custom-call(bf16[4,576,128]{2,1,0:T(8,128)(2,1)} %bitcast.4, bf16[2,576,128]{2,1,0:T(8,128)(2,1)} %bitcast.5, bf16[4,576]{1,0:T(4,128)(2,1)} %fresh_ref.1, s32[2]{0:T(128)} %lengths_ref.1, bf16[4,3584]{1,0:T(4,128)(2,1)} %resid_ref.1, f32[3584]{0:T(1024)} %gain_ref.1, s32[4,8]{1,0:T(4,128)} %ids_ref.1, ...), custom_call_target="tpu_custom_call" | custom-call | tf_op jit(solution)/shard_map/pallas_call | solution.py:464
  64.4 1.4 %copy.20 = bf16[4,3584]{1,0:T(4,128)(2,1)} copy(bf16[4,3584]{1,0:T(4,128)(2,1)} %shard_map.172) | data formatting | bytes 57344

commit v4 on v3

--- a/solution.py
+++ b/solution.py
@@ -115,9 +115,16 @@
             lat_send.at[d], lat_recv.at[slot], lat_ss, lat_rs.at[z], d // sides, d % sides
         )
 
-    @pl.loop(1, n)
+    near, inside = me // (n // 2) * (n // 2), me % (n // 2)
+    far = n // 2 - near
+
+    @pl.loop(0, n // 2)
     def _(k):
-        lat_copy((me + (k * 13) % n) % n, me).start()
+        lat_copy(far + (inside + k * 5) % (n // 2), me).start()
+
+    @pl.loop(1, n // 2)
+    def _(k):
+        lat_copy(near + (inside + k * 5) % (n // 2), me).start()
 
     lat_recv[me] = lat_send[me]
 

time: 65.9 us -> 66.5 us (level)
  Pallas kernels: 64.3 us -> 65 us
where the time goes in v4:
time: 66.5 us; the launch traced here: 66.3 us
  Pallas kernels  65 us (98%)
  local copies, waits for them, and re-layouts  1.37 us (2%)
    pallas_call x1, Pallas kernels, local(): pl.pallas_call(body, out_shape=jax.ShapeDtypeStruct((tok, feature), BF),...  65 us
    unnamed x1, local copies, waits for them, and re-layouts  1.37 us

profile of v4, /device:TPU:0, one launch (start us, length us, event | category | flops | bytes accessed | tf_op | source)
XLA Modules:
  0.0 66.3 jit_solution(7348814495974646920)
XLA Ops:
  0.0 65.0 %shard_map.172 = bf16[4,3584]{1,0:T(4,128)(2,1)} custom-call(bf16[4,576,128]{2,1,0:T(8,128)(2,1)} %bitcast.4, bf16[2,576,128]{2,1,0:T(8,128)(2,1)} %bitcast.5, bf16[4,576]{1,0:T(4,128)(2,1)} %fresh_ref.1, s32[2]{0:T(128)} %lengths_ref.1, bf16[4,3584]{1,0:T(4,128)(2,1)} %resid_ref.1, f32[3584]{0:T(1024)} %gain_ref.1, s32[4,8]{1,0:T(4,128)} %ids_ref.1, ...), custom_call_target="tpu_custom_call" | custom-call | tf_op jit(solution)/shard_map/pallas_call | solution.py:471
  65.0 1.4 %copy.20 = bf16[4,3584]{1,0:T(4,128)(2,1)} copy(bf16[4,3584]{1,0:T(4,128)(2,1)} %shard_map.172) | data formatting | bytes 57344
